TPU v7x, 256 devices: a whole 4x4x8 slice. The times are simulated.
256 devices in a mesh: ax: 32 (over x, y, core), th: 8 (over z).
Axes of the slice: x: 4, y: 4, z: 8, core: 2. Of those that a mesh axis runs over, the one named last changes fastest.
Arguments:
- populations: float32 [26, 16, 64, 4096], P(None, None, 'th', 'ax')
- wall_free: float32 [128, 262144], P(None, ('ax', 'th')), may hold values from 0 to 1
- wall_bound: float32 [128, 262144], P(None, ('ax', 'th')), may hold values from 0 to 0.5
- wall_propagator: float32 [128, 128], replicated
- bind_on: float32 [128], replicated, may hold values from 0.02 to 0.2
- bind_off: float32 [128], replicated, may hold values from 0.02 to 0.2
- iface_sector: int32 [262144, 1], P(('ax', 'th')), may hold values from 0 to 7; in each aligned block of 1024 rows (0 to 1023, 1024 to 2047, ...) at most 256 rows name the same one
- iface_line: int32 [262144], P(('ax', 'th')), may hold values from 0 to 1023
- strut_mask: int32 [262144], P(('ax', 'th')), may hold values 0 or 1
Outputs:
- drug_field: float32 [16, 64, 4096], P(None, 'th', 'ax')
- axial_flow: float32 [16, 64, 4096], P(None, 'th', 'ax')
- free_drug: float32 [128, 262144], P(None, ('ax', 'th'))
- bound_drug: float32 [128, 262144], P(None, ('ax', 'th'))
Inputs may be any that keep to these rules, and one draw needn't show every extreme that they name: `iface_sector`: among the rows of one device at most 256 name one sector, and in some device exactly 256 do.
All inputs are finite; a program needn't handle non-finite values. No bound on the sum of `strut_mask` on one device may be relied on, other than what follows from the above.
Results may differ from a plain program's by a relative error of at most 0.00023.
Values sent between devices are 32-bit elements; how exact they have to be, the bound alone decides.
A program may use at most 64 MiB of HBM per device.

v0:
```python
import functools

import jax
import jax.numpy as jnp
from jax import lax
from jax.experimental import pallas as pl
from jax.experimental.pallas import tpu as pltpu
from jax.sharding import PartitionSpec as P

STEPS = 4
RELAX_FLOW = 1.25
RELAX_DRUG = 1.1
PUSH_AXIAL = 0.0001
PERMEABILITY = 0.3
RELEASE_RATE = 0.5

VELOCITIES = [
    (0, 0, 0), (1, 0, 0), (-1, 0, 0), (0, 1, 0), (0, -1, 0), (0, 0, 1), (0, 0, -1),
    (1, 1, 0), (-1, -1, 0), (1, -1, 0), (-1, 1, 0), (1, 0, 1), (-1, 0, -1),
    (1, 0, -1), (-1, 0, 1), (0, 1, 1), (0, -1, -1), (0, 1, -1), (0, -1, 1),
    (0, 0, 0), (1, 0, 0), (-1, 0, 0), (0, 1, 0), (0, -1, 0), (0, 0, 1), (0, 0, -1),
]
OPPOSITE = [0, 2, 1, 4, 3, 6, 5, 8, 7, 10, 9, 12, 11, 14, 13, 16, 15, 18, 17, 19, 21, 20, 23, 22, 25, 24]
MIRROR = [0, 1, 2, 3, 4, 6, 5, 7, 8, 9, 10, 13, 14, 11, 12, 17, 18, 15, 16, 19, 20, 21, 22, 23, 25, 24]

S_UP = [3, 7, 10, 15, 17, 22]
S_DOWN = [4, 8, 9, 16, 18, 23]
MOVING = S_UP + S_DOWN
STILL = [q for q in range(26) if q not in MOVING]
Z_UP = [1, 7, 9, 11, 13, 20]
Z_DOWN = [2, 8, 10, 12, 14, 21]

F32 = jnp.float32
BF16 = jnp.bfloat16
MESH = pl.DeviceIdType.MESH


def wait_bytes(ref, sem):
    pltpu.make_async_copy(ref, ref, sem).wait()


def kernel(
    pops, free_in, bound_in, prop, on_row, off_row, sector, line, strut,
    drug_out, axial_out, free, bound,
    moving, still, drug_top, drug_now, speed_top, packed, faces, tops,
    onehot_hi, onehot_lo, lanes_lo, code_in, open_row, line_open, line_count, line_strut,
    table, sums, fixed_out, fixed_in, source,
    wide, from_source, to_surface, on_wide, off_wide, substep, propagated,
    table_send, table_recv, sums_send, sums_recv, fixed_send, fixed_recv,
    flow_send, flow_recv, top_send, top_recv,
):
    n_ax, n_th = lax.axis_size("ax"), lax.axis_size("th")
    ax, th = lax.axis_index("ax"), lax.axis_index("th")
    radial = pops.shape[1]
    top = radial - 1
    lane = lax.broadcasted_iota(jnp.int32, (8, 128), 1)
    ax_up, ax_down = lax.rem(ax + 1, n_ax), lax.rem(ax + n_ax - 1, n_ax)
    th_up, th_down = lax.rem(th + 1, n_th), lax.rem(th + n_th - 1, n_th)

    def peer(offset):
        return (ax, lax.rem(th + offset, n_th))

    beside = [
        (ax_up, th), (ax_down, th),
        (ax_up, th_up), (ax_up, th_down), (ax_down, th_up), (ax_down, th_down),
    ]
    barrier = pltpu.get_barrier_semaphore()
    greeted = [peer(o) for o in range(1, n_th)] + beside
    for device in greeted:
        pl.semaphore_signal(barrier, inc=1, device_id=device, device_id_type=MESH)

    relative = lax.rem(sector[...] - th + n_th, n_th)
    line_all = line[...]
    line_lo = jnp.bitwise_and(line_all, 127)
    line_hi = jnp.right_shift(line_all, 7)
    code_out = relative * 8 + line_hi
    lanes_lo[...] = line_lo
    code_in[...] = lax.rem(n_th - relative, n_th) * 8 + line_hi
    n_blocks = 8 * n_th
    down_blocks = lax.broadcasted_iota(jnp.int32, (n_blocks, 128), 0)
    down_lanes = lax.broadcasted_iota(jnp.int32, (128, 128), 0)
    for s in range(8):
        part = pl.ds(128 * s, 128)
        onehot_hi[:, part] = jnp.where(down_blocks == code_out[s : s + 1, :], 1.0, 0.0).astype(BF16)
        onehot_lo[:, part] = jnp.where(down_lanes == line_lo[s : s + 1, :], 1.0, 0.0).astype(BF16)

    def by_line(values):
        high = values.astype(BF16).astype(F32)
        low = values - high
        total = None
        for s in range(0, 8, 2):
            part = pl.ds(128 * s, 256)
            ones = onehot_hi[:, part]
            rows = []
            for piece in (high, low):
                row = jnp.concatenate([piece[s : s + 1, :], piece[s + 1 : s + 2, :]], axis=1)
                rows.append(ones * row.astype(BF16))
            term = lax.dot_general(
                jnp.concatenate(rows, axis=0),
                onehot_lo[:, part],
                (((1,), (1,)), ((), ())),
                preferred_element_type=F32,
            )
            total = term if total is None else total + term
        return total[:n_blocks] + total[n_blocks:]

    def gathered(block):
        result = jnp.zeros((8, 128), F32)
        where = lanes_lo[...]
        code = code_in[...]
        for o in range(n_th):
            for hi in range(8):
                row = jnp.broadcast_to(block(o, hi), (8, 128))
                found = jnp.take_along_axis(row, where, axis=1, mode="promise_in_bounds")
                result = jnp.where(code == o * 8 + hi, found, result)
        return result

    def table_copy(t, o):
        return pltpu.make_async_remote_copy(
            table.at[t, 0], table.at[t, o], table_send.at[t], table_recv.at[t], peer(o), MESH
        )

    def sums_copy(t, o):
        return pltpu.make_async_remote_copy(
            sums.at[0, t, o], sums.at[1, t, o], sums_send.at[t], sums_recv.at[t], peer(o), MESH
        )

    def fixed_copy(o):
        return pltpu.make_async_remote_copy(
            fixed_out.at[o], fixed_in.at[o], fixed_send, fixed_recv, peer(o), MESH
        )

    def send_sums(t, surface):
        found = by_line(surface)
        for o in range(n_th):
            sums[0, t, o] = found[8 * o : 8 * o + 8]
        for o in range(1, n_th):
            sums_copy(t, o).start()

    for c in range(8):
        table[0, 0, c : c + 1, :] = free_in[0:1, 128 * c : 128 * c + 128]
    strut_own = strut[...].astype(F32)
    counts = by_line(jnp.ones((8, 128), F32))
    for o in range(n_th):
        fixed_out[o, 0] = strut_own
        fixed_out[o, 1] = counts[8 * o : 8 * o + 8]
    surface = pops[19, top]
    for q in range(20, 26):
        surface = surface + pops[q, top]
    for q in range(19, 26):
        drug_now[q - 19] = pops[q, top]
    drug_now[7] = surface
    pl.semaphore_wait(barrier, len(greeted))
    for o in range(1, n_th):
        fixed_copy(o).start()
        table_copy(0, o).start()
    send_sums(0, surface)

    prop_all = prop[...]
    prop_hi = prop_all.astype(BF16)
    prop_lo = (prop_all - prop_hi.astype(F32)).astype(BF16)
    wide[...] = jnp.concatenate([prop_hi, prop_lo, prop_hi], axis=1)
    from_source[...] = jnp.broadcast_to(prop_all[:, 0:1], (128, 128))
    to_surface[...] = jnp.transpose(jnp.broadcast_to(prop_all[0:1, :], (128, 128)))
    on_wide[...] = jnp.transpose(jnp.broadcast_to(on_row[...], (128, 128)))
    off_wide[...] = jnp.transpose(jnp.broadcast_to(off_row[...], (128, 128)))
    bound[...] = bound_in[...]
    WIDTH = 256
    LINES_OWN = free_in.shape[1]

    def diffuse(x):
        x_hi = x.astype(BF16)
        x_lo = (x - x_hi.astype(F32)).astype(BF16)
        return jnp.dot(
            wide[...], jnp.concatenate([x_hi, x_hi, x_lo], axis=0), preferred_element_type=F32
        )

    for c in range(0, LINES_OWN, WIDTH):
        propagated[:, c : c + WIDTH] = diffuse(free_in[:, c : c + WIDTH])

    def own(p, q, r):
        if q in S_UP:
            return moving.at[p, MOVING.index(q), r, 8:16, :]
        if q in S_DOWN:
            return moving.at[p, MOVING.index(q), r, 0:8, :]
        return still.at[p, STILL.index(q), r]

    def shifted_s(p, q, r):
        if q in S_UP:
            return moving[p, MOVING.index(q), r, 7:15, :]
        if q in S_DOWN:
            return moving[p, MOVING.index(q), r, 1:9, :]
        return still[p, STILL.index(q), r]

    def rotation(shift):
        return shift % 128 if isinstance(shift, int) else lax.rem(shift, 128)

    def pulled(t, p, q, r):
        value = shifted_s(p, q, r)
        step_z, step_s, _ = VELOCITIES[q]
        if step_z == 0:
            return value
        first = 8 - step_s
        if step_z == 1:
            face = faces[t, 0, first : first + 8, :]
            slot = Z_UP.index(q) * 16 + r
            face = pltpu.roll(face, rotation(128 - slot), 1)
            return jnp.where(lane == 0, face, pltpu.roll(value, 1, 1))
        face = faces[t, 1, first : first + 8, :]
        slot = Z_DOWN.index(q) * 16 + r
        face = pltpu.roll(face, rotation(127 - slot), 1)
        return jnp.where(lane == 127, face, pltpu.roll(value, 127, 1))

    def moved(t, p, q, r, where):
        step_r = VELOCITIES[q][2]
        if step_r == 1 and where == "bottom":
            return pulled(t, p, MIRROR[q], r)
        if step_r == -1 and where == "top":
            return own(p, OPPOSITE[q], r)[...]
        return pulled(t, p, q, r - step_r)

    def collide_flow(f):
        d = {q: f[q] - f[q + 1] for q in (1, 3, 5, 7, 9, 11, 13, 15, 17)}
        density = f[0]
        for q in range(1, 19):
            density = density + f[q]
        jz = d[1] + d[7] + d[9] + d[11] + d[13] + PUSH_AXIAL
        js = d[3] + d[7] - d[9] + d[15] + d[17]
        jr = d[5] + d[11] - d[13] + d[15] - d[17]
        uz, us, ur = jz / density, js / density, jr / density
        base = 1.0 - 1.5 * (uz * uz + us * us + ur * ur)
        edge = density * (RELAX_FLOW / 36.0)
        face = density * (RELAX_FLOW / 18.0)
        keep = 1.0 - RELAX_FLOW
        post = {0: keep * f[0] + density * (RELAX_FLOW / 3.0) * base}
        along = {
            1: uz, 3: us, 5: ur, 7: uz + us, 9: uz - us,
            11: uz + ur, 13: uz - ur, 15: us + ur, 17: us - ur,
        }
        for q, speed in along.items():
            weight = face if q < 7 else edge
            even = weight * (base + 4.5 * speed * speed)
            odd = weight * (3.0 * speed)
            post[q] = keep * f[q] + (even + odd)
            post[q + 1] = keep * f[q + 1] + (even - odd)
        return post, (uz, us, ur)

    def collide_drug(f, total, speeds):
        keep = 1.0 - RELAX_DRUG
        share = total * (RELAX_DRUG * 0.125)
        post = {19: keep * f[19] + 2.0 * share}
        for q, speed in zip((20, 22, 24), speeds):
            odd = 4.0 * speed
            post[q] = keep * f[q] + share * (1.0 + odd)
            post[q + 1] = keep * f[q + 1] + share * (1.0 - odd)
        return post

    def pack(post, r, packs):
        up, down = packs
        for k, q in enumerate(Z_UP):
            if q in post:
                slot = 16 * k + r
                up = jnp.where(lane == slot, pltpu.roll(post[q], rotation(slot + 1), 1), up)
        for k, q in enumerate(Z_DOWN):
            if q in post:
                slot = 16 * k + r
                down = jnp.where(lane == slot, pltpu.roll(post[q], rotation(slot), 1), down)
        return up, down

    def layer(read, p, r, packs, where):
        f = {q: read(q, r, where) for q in range(19 if where == "top" else 26)}
        post, speeds = collide_flow(f)
        if where == "top":
            for i in range(3):
                speed_top[i] = speeds[i]
        else:
            total = f[19]
            for q in range(20, 26):
                total = total + f[q]
            post.update(collide_drug(f, total, speeds))
        for q, value in post.items():
            own(p, q, r)[...] = value
        return pack(post, r, packs)

    def flow_copies(t, p):
        def copy(src, dst, device, i):
            return pltpu.make_async_remote_copy(
                src, dst, flow_send.at[t, i], flow_recv.at[t, i], device, MESH
            )

        up, down = (ax, th_up), (ax, th_down)
        copies = [
            copy(moving.at[p, 0:5, :, 15, :], moving.at[p, 0:5, :, 7, :], up, 0),
            copy(moving.at[p, 6:11, :, 0, :], moving.at[p, 6:11, :, 8, :], down, 1),
            copy(moving.at[p, 5, 0:top, 15, :], moving.at[p, 5, 0:top, 7, :], up, 2),
            copy(moving.at[p, 11, 0:top, 0, :], moving.at[p, 11, 0:top, 8, :], down, 3),
        ]
        for side, to in ((0, ax_up), (1, ax_down)):
            i = 4 + 3 * side
            copies += [
                copy(packed.at[t, side], faces.at[t, side, 8:16, :], (to, th), i),
                copy(packed.at[t, side, 7:8, :], faces.at[t, side, 7:8, :], (to, th_up), i + 1),
                copy(packed.at[t, side, 0:1, :], faces.at[t, side, 16:17, :], (to, th_down), i + 2),
            ]
        return copies

    def collide_all(t, p, read, bottom):
        packs = (jnp.zeros((8, 128), F32), jnp.zeros((8, 128), F32))
        if bottom:
            packs = layer(read, p, 0, packs, "bottom")
        packs = lax.fori_loop(
            1 if bottom else 0, top, lambda r, packs: layer(read, p, r, packs, "middle"), packs
        )
        up, down = layer(read, p, top, packs, "top")
        packed[t, 0] = up
        packed[t, 1] = down
        for copy in flow_copies(t, p):
            copy.start()

    def top_copies(t, p):
        def copy(src, dst, device, i):
            return pltpu.make_async_remote_copy(
                src, dst, top_send.at[t, i], top_recv.at[t, i], device, MESH
            )

        return [
            copy(drug_top.at[p, 1, 0:8, :], tops.at[t, 0], (ax_up, th), 0),
            copy(drug_top.at[p, 2, 0:8, :], tops.at[t, 1], (ax_down, th), 1),
            copy(drug_top.at[p, 3, 15, :], drug_top.at[p, 3, 7, :], (ax, th_up), 2),
            copy(drug_top.at[p, 4, 0, :], drug_top.at[p, 4, 8, :], (ax, th_down), 3),
        ]

    def wall_flux(t, p):
        wait_bytes(table.at[t, pl.ds(1, n_th - 1)], table_recv.at[t])
        free_rows = gathered(lambda o, hi: table[t, o, hi : hi + 1, :])
        surface = drug_now[7]
        flux = open_row[...] * (surface - free_rows)
        lowered = {19: drug_now[0] - 0.25 * flux}
        for q in range(20, 26):
            lowered[q] = drug_now[q - 19] - 0.125 * flux
        post = collide_drug(lowered, surface - flux, [speed_top[i] for i in range(3)])
        drug_top[p, 1, 0:8, :] = post[20]
        drug_top[p, 2, 0:8, :] = post[21]
        drug_top[p, 3, 8:16, :] = post[22]
        drug_top[p, 4, 0:8, :] = post[23]
        for copy in top_copies(t, p):
            copy.start()
        drug_top[p, 0, 0:8, :] = post[19]
        drug_top[p, 5, 0:8, :] = post[24]
        own(p, 25, top)[...] = post[25]

    def react(x, b, on, off):
        rate = on * x * (1.0 - b) - off * b
        return x - rate, b + rate

    def wall_first(t, send):
        wait_bytes(sums.at[1, t, pl.ds(1, n_th - 1)], sums_recv.at[t])
        total = sums[0, t, 0]
        for o in range(1, n_th):
            total = total + sums[1, t, o]
        flux = line_open[...] * (total - line_count[...] * table[t, 0])
        source[...] = flux + RELEASE_RATE * line_strut[...]
        for c in range(8):
            part = pl.ds(128 * c, 128)
            x = propagated[:, part] + from_source[...] * source[c : c + 1, :]
            x, b = react(x, bound[:, part], on_wide[...], off_wide[...])
            substep[:, part] = x
            bound[:, part] = b
            if send:
                x = jnp.sum(to_surface[...] * x, axis=0, keepdims=True)
                x, _ = react(x, b[0:1, :], on_wide[0:1, :], off_wide[0:1, :])
                table[t + 1, 0, c : c + 1, :] = x
        if send:
            for o in range(1, n_th):
                table_copy(t + 1, o).start()

    def wall_second(last):
        wide_on = jnp.concatenate([on_wide[...]] * (WIDTH // 128), axis=1)
        wide_off = jnp.concatenate([off_wide[...]] * (WIDTH // 128), axis=1)
        for c in range(0, LINES_OWN, WIDTH):
            part = pl.ds(c, WIDTH)
            x, b = react(diffuse(substep[:, part]), bound[:, part], wide_on, wide_off)
            bound[:, part] = b
            if last:
                free[:, part] = x
            else:
                propagated[:, part] = diffuse(x)

    def top_moved(t, p):
        f = {19: drug_top[p, 0, 0:8, :]}
        f[20] = jnp.where(lane == 0, pltpu.roll(tops[t, 0], 1, 1), pltpu.roll(drug_top[p, 1, 0:8, :], 1, 1))
        f[21] = jnp.where(lane == 127, pltpu.roll(tops[t, 1], 127, 1), pltpu.roll(drug_top[p, 2, 0:8, :], 127, 1))
        f[22] = drug_top[p, 3, 7:15, :]
        f[23] = drug_top[p, 4, 1:9, :]
        f[24] = own(p, 24, top - 1)[...]
        f[25] = drug_top[p, 5, 0:8, :]
        total = f[19]
        for q in range(20, 26):
            total = total + f[q]
        return f, total

    def wait_tops(t, p):
        for copy in top_copies(t, p):
            copy.wait()

    def wait_flow(t, p):
        for copy in flow_copies(t, p):
            copy.wait()

    def wait_coupling_sends(t):
        wait_bytes(table.at[t, pl.ds(1, n_th - 1)], table_send.at[t])
        wait_bytes(sums.at[1, t, pl.ds(1, n_th - 1)], sums_send.at[t])

    collide_all(0, 0, lambda q, r, where: pops[q, r], False)
    wait_bytes(fixed_in.at[pl.ds(1, n_th - 1)], fixed_recv)
    line_strut[...] = strut_own
    line_open[...] = PERMEABILITY * (1.0 - strut_own)
    count = fixed_out[0, 1]
    for o in range(1, n_th):
        count = count + fixed_in[o, 1]
    line_count[...] = count
    fixed_in[0, 0] = strut_own
    covered = gathered(lambda o, hi: fixed_in[o, 0, hi : hi + 1, :])
    open_row[...] = PERMEABILITY * (1.0 - covered)
    wait_bytes(fixed_in.at[pl.ds(1, n_th - 1)], fixed_send)

    def step(t, carry):
        p = lax.rem(t, 2)
        wall_flux(t, p)
        wall_first(t, True)
        wall_second(False)
        wait_coupling_sends(t)
        wait_flow(t, p)
        collide_all(t + 1, 1 - p, lambda q, r, where: moved(t, p, q, r, where), True)
        wait_tops(t, p)
        f, total = top_moved(t, p)
        for q in range(19, 26):
            drug_now[q - 19] = f[q]
        drug_now[7] = total
        send_sums(t + 1, total)
        return carry

    lax.fori_loop(0, STEPS - 1, step, 0)

    t, p = STEPS - 1, (STEPS - 1) % 2
    wall_flux(t, p)
    wait_flow(t, p)

    def result(r, where):
        f = {q: moved(t, p, q, r, where) for q in Z_UP[:5] + Z_DOWN[:5]}
        flow = None
        for q in Z_UP[:5]:
            term = f[q] - f[OPPOSITE[q]]
            flow = term if flow is None else flow + term
        axial_out[r] = flow
        if where != "top":
            total = moved(t, p, 19, r, where)
            for q in range(20, 26):
                total = total + moved(t, p, q, r, where)
            drug_out[r] = total

    def result_middle(r, carry):
        result(r, "middle")
        return carry

    result(0, "bottom")
    lax.fori_loop(1, top, result_middle, 0)
    result(top, "top")
    wall_first(t, False)
    wall_second(True)
    wait_coupling_sends(t)
    wait_tops(t, p)
    drug_out[top] = top_moved(t, p)[1]


def per_device(
    populations, wall_free, wall_bound, wall_propagator, bind_on, bind_off,
    iface_sector, iface_line, strut_mask,
):
    n_th = lax.axis_size("th")
    radial = populations.shape[1]
    vmem = pl.BlockSpec(memory_space=pltpu.VMEM)
    block = (8, 128)
    scratch = [
        pltpu.VMEM((2, len(MOVING), radial, 16, 128), F32),
        pltpu.VMEM((2, len(STILL), radial, 8, 128), F32),
        pltpu.VMEM((2, 6, 16, 128), F32),
        pltpu.VMEM((8, *block), F32),
        pltpu.VMEM((3, *block), F32),
        pltpu.VMEM((STEPS, 2, *block), F32),
        pltpu.VMEM((STEPS, 2, 24, 128), F32),
        pltpu.VMEM((STEPS, 2, *block), F32),
        pltpu.VMEM((8 * n_th, 1024), BF16),
        pltpu.VMEM((128, 1024), BF16),
        pltpu.VMEM(block, jnp.int32),
        pltpu.VMEM(block, jnp.int32),
        pltpu.VMEM(block, F32),
        pltpu.VMEM(block, F32),
        pltpu.VMEM(block, F32),
        pltpu.VMEM(block, F32),
        pltpu.VMEM((STEPS, n_th, *block), F32),
        pltpu.VMEM((2, STEPS, n_th, *block), F32),
        pltpu.VMEM((n_th, 2, *block), F32),
        pltpu.VMEM((n_th, 2, *block), F32),
        pltpu.VMEM(block, F32),
        pltpu.VMEM((128, 384), BF16),
        pltpu.VMEM((128, 128), F32),
        pltpu.VMEM((128, 128), F32),
        pltpu.VMEM((128, 128), F32),
        pltpu.VMEM((128, 128), F32),
        pltpu.VMEM((128, 1024), F32),
        pltpu.VMEM((128, 1024), F32),
        pltpu.SemaphoreType.DMA((STEPS,)),
        pltpu.SemaphoreType.DMA((STEPS,)),
        pltpu.SemaphoreType.DMA((STEPS,)),
        pltpu.SemaphoreType.DMA((STEPS,)),
        pltpu.SemaphoreType.DMA,
        pltpu.SemaphoreType.DMA,
        pltpu.SemaphoreType.DMA((STEPS, 10)),
        pltpu.SemaphoreType.DMA((STEPS, 10)),
        pltpu.SemaphoreType.DMA((STEPS, 4)),
        pltpu.SemaphoreType.DMA((STEPS, 4)),
    ]
    field = jax.ShapeDtypeStruct((radial, *block), F32)
    wall = jax.ShapeDtypeStruct(wall_free.shape, F32)
    return pl.pallas_call(
        kernel,
        out_shape=(field, field, wall, wall),
        in_specs=[vmem] * 9,
        out_specs=(vmem,) * 4,
        scratch_shapes=scratch,
        compiler_params=pltpu.CompilerParams(
            collective_id=0, has_side_effects=True, vmem_limit_bytes=40 * 2**20
        ),
    )(
        populations, wall_free, wall_bound, wall_propagator,
        bind_on.reshape(1, 128), bind_off.reshape(1, 128),
        iface_sector.reshape(block), iface_line.reshape(block), strut_mask.reshape(block),
    )


def solution(mesh):
    cells = P(None, "th", "ax")
    lines = P(None, ("ax", "th"))
    return jax.shard_map(
        per_device,
        mesh=mesh,
        in_specs=(
            P(None, None, "th", "ax"), lines, lines, P(), P(), P(),
            P(("ax", "th"), None), P(("ax", "th")), P(("ax", "th")),
        ),
        out_specs=(cells, cells, lines, lines),
        check_vma=False,
    )
```

profile of v0, /device:TPU:1, one launch (start us, length us, event | category | flops | bytes accessed | tf_op | source)
XLA Modules:
  0.0 59.0 jit_solution(11681654271993102665)
XLA Ops:
  0.6 0.0 copy-start
  0.6 1.4 %copy-done = f32[26,16,8,128]{3,2,1,0:T(8,128)S(1)} copy-done((f32[26,16,8,128]{3,2,1,0:T(8,128)S(1)}, f32[26,16,8,128]{3,2,1,0:T(8,128)}, u32[]{:S(2)}) %copy-start) | copy-done | bytes 1703960
  2.1 0.0 copy-start.1
  2.1 1.0 %copy-done.1 = f32[128,1024]{1,0:T(8,128)S(1)} copy-done((f32[128,1024]{1,0:T(8,128)S(1)}, f32[128,1024]{1,0:T(8,128)}, u32[]{:S(2)}) %copy-start.1) | copy-done | bytes 524312
  3.1 0.0 copy-start.2
  3.1 1.0 %copy-done.2 = f32[128,1024]{1,0:T(8,128)S(1)} copy-done((f32[128,1024]{1,0:T(8,128)S(1)}, f32[128,1024]{1,0:T(8,128)}, u32[]{:S(2)}) %copy-start.2) | copy-done | bytes 524312
  4.2 0.0 copy-start.3
  4.2 0.8 %copy-done.3 = f32[128,128]{1,0:T(8,128)S(1)} copy-done((f32[128,128]{1,0:T(8,128)S(1)}, f32[128,128]{1,0:T(8,128)}, u32[]{:S(2)}) %copy-start.3) | copy-done | bytes 65560
  5.0 0.0 copy-start.4
  5.0 0.7 %copy-done.4 = s32[1024,1]{0,1:T(1,128)S(1)} copy-done((s32[1024,1]{0,1:T(1,128)S(1)}, s32[1024,1]{0,1:T(1,128)}, u32[]{:S(2)}) %copy-start.4) | copy-done | bytes 4120
  5.7 0.0 copy-start.5
  5.7 0.7 %copy-done.5 = s32[1024]{0:T(1024)S(1)} copy-done((s32[1024]{0:T(1024)S(1)}, s32[1024]{0:T(1024)}, u32[]{:S(2)}) %copy-start.5) | copy-done | bytes 4120
  6.4 0.0 copy-start.6
  6.4 0.7 %copy-done.6 = s32[1024]{0:T(1024)S(1)} copy-done((s32[1024]{0:T(1024)S(1)}, s32[1024]{0:T(1024)}, u32[]{:S(2)}) %copy-start.6) | copy-done | bytes 4120
  7.1 0.0 copy-start.7
  7.1 0.7 %copy-done.7 = f32[128]{0:T(128)S(1)} copy-done((f32[128]{0:T(128)S(1)}, f32[128]{0:T(128)}, u32[]{:S(2)}) %copy-start.7) | copy-done | bytes 536
  7.7 0.0 copy-start.8
  7.7 0.7 %copy-done.8 = f32[128]{0:T(128)S(1)} copy-done((f32[128]{0:T(128)S(1)}, f32[128]{0:T(128)}, u32[]{:S(2)}) %copy-start.8) | copy-done | bytes 536
  8.4 47.8 %shard_map.120 = (f32[16,8,128]{2,1,0:T(8,128)S(1)}, f32[16,8,128]{2,1,0:T(8,128)S(1)}, f32[128,1024]{1,0:T(8,128)S(1)}, f32[128,1024]{1,0:T(8,128)S(1)}) custom-call(f32[26,16,8,128]{3,2,1,0:T(8,128)S(1)} %copy-done, f32[128,1024]{1,0:T(8,128)S(1)} %copy-done.1, f32[128,1024]{1,0:T(8,128)S(1)} %copy-done.2, f32[128,128]{1,0:T(8,128)S(1)} %copy-done.3, ...), custom_call_target="tpu_custom_call" | custom-call | tf_op jit(solution)/shard_map/pallas_call | solution.py:526
  56.2 0.6 %copy.17 = f32[16,8,128]{2,1,0:T(8,128)} copy(f32[16,8,128]{2,1,0:T(8,128)S(1)} %get-tuple-element.8) | data formatting | bytes 131072
  56.8 0.6 %copy.18 = f32[16,8,128]{2,1,0:T(8,128)} copy(f32[16,8,128]{2,1,0:T(8,128)S(1)} %get-tuple-element.9) | data formatting | bytes 131072
  57.4 0.8 %copy.19 = f32[128,1024]{1,0:T(8,128)} copy(f32[128,1024]{1,0:T(8,128)S(1)} %get-tuple-element.10) | data formatting | bytes 1048576
  58.2 0.8 %copy.20 = f32[128,1024]{1,0:T(8,128)} copy(f32[128,1024]{1,0:T(8,128)S(1)} %get-tuple-element.11) | data formatting | bytes 1048576
Async XLA Ops:
  0.6 1.5 %copy-start = (f32[26,16,8,128]{3,2,1,0:T(8,128)S(1)}, f32[26,16,8,128]{3,2,1,0:T(8,128)}, u32[]{:S(2)}) copy-start(f32[26,16,8,128]{3,2,1,0:T(8,128)} %pops.1) | copy-start | bytes 5111812
  2.1 1.0 %copy-start.1 = (f32[128,1024]{1,0:T(8,128)S(1)}, f32[128,1024]{1,0:T(8,128)}, u32[]{:S(2)}) copy-start(f32[128,1024]{1,0:T(8,128)} %free_in.1) | copy-start | bytes 1572868
  3.1 1.0 %copy-start.2 = (f32[128,1024]{1,0:T(8,128)S(1)}, f32[128,1024]{1,0:T(8,128)}, u32[]{:S(2)}) copy-start(f32[128,1024]{1,0:T(8,128)} %bound_in.1) | copy-start | bytes 1572868
  4.2 0.8 %copy-start.3 = (f32[128,128]{1,0:T(8,128)S(1)}, f32[128,128]{1,0:T(8,128)}, u32[]{:S(2)}) copy-start(f32[128,128]{1,0:T(8,128)} %prop.1) | copy-start | bytes 196612
  5.0 0.7 %copy-start.4 = (s32[1024,1]{0,1:T(1,128)S(1)}, s32[1024,1]{0,1:T(1,128)}, u32[]{:S(2)}) copy-start(s32[1024,1]{0,1:T(1,128)} %param.15) | copy-start | bytes 12292
  5.7 0.7 %copy-start.5 = (s32[1024]{0:T(1024)S(1)}, s32[1024]{0:T(1024)}, u32[]{:S(2)}) copy-start(s32[1024]{0:T(1024)} %param.16) | copy-start | bytes 12292
  6.4 0.7 %copy-start.6 = (s32[1024]{0:T(1024)S(1)}, s32[1024]{0:T(1024)}, u32[]{:S(2)}) copy-start(s32[1024]{0:T(1024)} %param.17) | copy-start | bytes 12292
  7.1 0.7 %copy-start.7 = (f32[128]{0:T(128)S(1)}, f32[128]{0:T(128)}, u32[]{:S(2)}) copy-start(f32[128]{0:T(128)} %param.13) | copy-start | bytes 1540
  7.7 0.7 %copy-start.8 = (f32[128]{0:T(128)S(1)}, f32[128]{0:T(128)}, u32[]{:S(2)}) copy-start(f32[128]{0:T(128)} %param.14) | copy-start | bytes 1540
where the time goes:
time: 59.4 us; the launch traced here: 59 us
  Pallas kernels  47.8 us (80%)
  local copies, waits for them, and re-layouts  10.6 us (18%)
  between operations  0.66 us (1%)
    pallas_call x1, Pallas kernels, per_device(): pl.pallas_call(kernel, out_shape=(field, field, wall, wall), in_specs=[vm...  47.8 us
    unnamed x22, local copies, waits for them, and re-layouts  10.6 us

commit v1 on v0

--- a/solution.py
+++ b/solution.py
@@ -35,17 +35,34 @@
 MESH = pl.DeviceIdType.MESH
 
 
+WIDTH = 256
+
+
+def diffuse(wide, x):
+    x_hi = x.astype(BF16)
+    x_lo = (x - x_hi.astype(F32)).astype(BF16)
+    return jnp.dot(
+        wide[...], jnp.concatenate([x_hi, x_hi, x_lo], axis=0), preferred_element_type=F32
+    )
+
+
+def react(x, b, on, off):
+    rate = on * x * (1.0 - b) - off * b
+    return x - rate, b + rate
+
+
 def wait_bytes(ref, sem):
     pltpu.make_async_copy(ref, ref, sem).wait()
 
 
 def kernel(
-    pops, free_in, bound_in, prop, on_row, off_row, sector, line, strut,
-    drug_out, axial_out, free, bound,
+    pops_hbm, free_hbm, bound_hbm, prop_hbm, on_hbm, off_hbm, sector_hbm, line_hbm, strut_hbm,
+    drug_out, axial_out, substep, bound, wide, on_wide, off_wide,
+    pops, free_in, prop, on_row, off_row, sector, line, strut, first_drug, first_free, load_sems,
     moving, still, drug_top, drug_now, speed_top, packed, faces, tops,
     onehot_hi, onehot_lo, lanes_lo, code_in, open_row, line_open, line_count, line_strut,
     table, sums, fixed_out, fixed_in, source,
-    wide, from_source, to_surface, on_wide, off_wide, substep, propagated,
+    from_source, to_surface, propagated,
     table_send, table_recv, sums_send, sums_recv, fixed_send, fixed_recv,
     flow_send, flow_recv, top_send, top_recv,
 ):
@@ -68,6 +85,20 @@
     greeted = [peer(o) for o in range(1, n_th)] + beside
     for device in greeted:
         pl.semaphore_signal(barrier, inc=1, device_id=device, device_id_type=MESH)
+
+    loads = [
+        (sector_hbm, sector), (line_hbm, line), (strut_hbm, strut),
+        (pops_hbm.at[19:26, top], first_drug), (free_hbm.at[0:8, :], first_free),
+        (prop_hbm, prop), (on_hbm, on_row), (off_hbm, off_row),
+        (free_hbm, free_in), (pops_hbm, pops), (bound_hbm, bound),
+    ]
+    loads = [
+        pltpu.make_async_copy(src, dst, load_sems.at[i]) for i, (src, dst) in enumerate(loads)
+    ]
+    for load in loads:
+        load.start()
+    for load in loads[:3]:
+        load.wait()
 
     relative = lax.rem(sector[...] - th + n_th, n_th)
     line_all = line[...]
@@ -137,18 +168,20 @@
         for o in range(1, n_th):
             sums_copy(t, o).start()
 
+    for load in loads[3:5]:
+        load.wait()
     for c in range(8):
-        table[0, 0, c : c + 1, :] = free_in[0:1, 128 * c : 128 * c + 128]
+        table[0, 0, c : c + 1, :] = first_free[0:1, 128 * c : 128 * c + 128]
     strut_own = strut[...].astype(F32)
     counts = by_line(jnp.ones((8, 128), F32))
     for o in range(n_th):
         fixed_out[o, 0] = strut_own
         fixed_out[o, 1] = counts[8 * o : 8 * o + 8]
-    surface = pops[19, top]
+    surface = first_drug[0]
     for q in range(20, 26):
-        surface = surface + pops[q, top]
+        surface = surface + first_drug[q - 19]
     for q in range(19, 26):
-        drug_now[q - 19] = pops[q, top]
+        drug_now[q - 19] = first_drug[q - 19]
     drug_now[7] = surface
     pl.semaphore_wait(barrier, len(greeted))
     for o in range(1, n_th):
@@ -156,6 +189,8 @@
         table_copy(0, o).start()
     send_sums(0, surface)
 
+    for load in loads[5:]:
+        load.wait()
     prop_all = prop[...]
     prop_hi = prop_all.astype(BF16)
     prop_lo = (prop_all - prop_hi.astype(F32)).astype(BF16)
@@ -164,19 +199,9 @@
     to_surface[...] = jnp.transpose(jnp.broadcast_to(prop_all[0:1, :], (128, 128)))
     on_wide[...] = jnp.transpose(jnp.broadcast_to(on_row[...], (128, 128)))
     off_wide[...] = jnp.transpose(jnp.broadcast_to(off_row[...], (128, 128)))
-    bound[...] = bound_in[...]
-    WIDTH = 256
-    LINES_OWN = free_in.shape[1]
-
-    def diffuse(x):
-        x_hi = x.astype(BF16)
-        x_lo = (x - x_hi.astype(F32)).astype(BF16)
-        return jnp.dot(
-            wide[...], jnp.concatenate([x_hi, x_hi, x_lo], axis=0), preferred_element_type=F32
-        )
-
-    for c in range(0, LINES_OWN, WIDTH):
-        propagated[:, c : c + WIDTH] = diffuse(free_in[:, c : c + WIDTH])
+    n_lines = free_in.shape[1]
+    for c in range(0, n_lines, WIDTH):
+        propagated[:, c : c + WIDTH] = diffuse(wide, free_in[:, c : c + WIDTH])
 
     def own(p, q, r):
         if q in S_UP:
@@ -349,10 +374,6 @@
         drug_top[p, 5, 0:8, :] = post[24]
         own(p, 25, top)[...] = post[25]
 
-    def react(x, b, on, off):
-        rate = on * x * (1.0 - b) - off * b
-        return x - rate, b + rate
-
     def wall_first(t, send):
         wait_bytes(sums.at[1, t, pl.ds(1, n_th - 1)], sums_recv.at[t])
         total = sums[0, t, 0]
@@ -374,17 +395,14 @@
             for o in range(1, n_th):
                 table_copy(t + 1, o).start()
 
-    def wall_second(last):
+    def wall_second():
         wide_on = jnp.concatenate([on_wide[...]] * (WIDTH // 128), axis=1)
         wide_off = jnp.concatenate([off_wide[...]] * (WIDTH // 128), axis=1)
-        for c in range(0, LINES_OWN, WIDTH):
+        for c in range(0, n_lines, WIDTH):
             part = pl.ds(c, WIDTH)
-            x, b = react(diffuse(substep[:, part]), bound[:, part], wide_on, wide_off)
+            x, b = react(diffuse(wide, substep[:, part]), bound[:, part], wide_on, wide_off)
             bound[:, part] = b
-            if last:
-                free[:, part] = x
-            else:
-                propagated[:, part] = diffuse(x)
+            propagated[:, part] = diffuse(wide, x)
 
     def top_moved(t, p):
         f = {19: drug_top[p, 0, 0:8, :]}
@@ -424,20 +442,24 @@
     open_row[...] = PERMEABILITY * (1.0 - covered)
     wait_bytes(fixed_in.at[pl.ds(1, n_th - 1)], fixed_send)
 
-    def step(t, carry):
-        p = lax.rem(t, 2)
-        wall_flux(t, p)
-        wall_first(t, True)
-        wall_second(False)
-        wait_coupling_sends(t)
-        wait_flow(t, p)
-        collide_all(t + 1, 1 - p, lambda q, r, where: moved(t, p, q, r, where), True)
+    def wall_side(t, p):
         wait_tops(t, p)
         f, total = top_moved(t, p)
         for q in range(19, 26):
             drug_now[q - 19] = f[q]
         drug_now[7] = total
         send_sums(t + 1, total)
+
+    def step(t, carry):
+        p = lax.rem(t, 2)
+        wall_flux(t, p)
+        wall_first(t, True)
+        pl.when(p == 1)(lambda: wall_side(t, p))
+        wall_second()
+        wait_coupling_sends(t)
+        wait_flow(t, p)
+        collide_all(t + 1, 1 - p, lambda q, r, where: moved(t, p, q, r, where), True)
+        pl.when(p == 0)(lambda: wall_side(t, p))
         return carry
 
     lax.fori_loop(0, STEPS - 1, step, 0)
@@ -467,10 +489,35 @@
     lax.fori_loop(1, top, result_middle, 0)
     result(top, "top")
     wall_first(t, False)
-    wall_second(True)
     wait_coupling_sends(t)
     wait_tops(t, p)
     drug_out[top] = top_moved(t, p)[1]
+
+
+def finish(
+    substep, bound_in, wide, on_wide, off_wide, drug_in, axial_in,
+    drug, axial, free, bound,
+    free_part, bound_part, sems,
+):
+    copies = [
+        pltpu.make_async_copy(drug_in, drug, sems.at[0]),
+        pltpu.make_async_copy(axial_in, axial, sems.at[1]),
+    ]
+    for copy in copies:
+        copy.start()
+    wide_on = jnp.concatenate([on_wide[...]] * (WIDTH // 128), axis=1)
+    wide_off = jnp.concatenate([off_wide[...]] * (WIDTH // 128), axis=1)
+    for i in range(substep.shape[1] // WIDTH):
+        part = pl.ds(i * WIDTH, WIDTH)
+        x, b = react(diffuse(wide, substep[:, part]), bound_in[:, part], wide_on, wide_off)
+        free_part[:, part] = x
+        bound_part[:, part] = b
+        for k, (src, dst) in enumerate(((free_part, free), (bound_part, bound))):
+            copy = pltpu.make_async_copy(src.at[:, part], dst.at[:, part], sems.at[2 + 2 * i + k])
+            copy.start()
+            copies.append(copy)
+    for copy in copies:
+        copy.wait()
 
 
 def per_device(
@@ -480,8 +527,21 @@
     n_th = lax.axis_size("th")
     radial = populations.shape[1]
     vmem = pl.BlockSpec(memory_space=pltpu.VMEM)
+    hbm = pl.BlockSpec(memory_space=pltpu.HBM)
     block = (8, 128)
+    wall_block = pltpu.VMEM(wall_free.shape, F32)
     scratch = [
+        pltpu.VMEM(populations.shape, F32),
+        wall_block,
+        pltpu.VMEM((128, 128), F32),
+        pltpu.VMEM((1, 128), F32),
+        pltpu.VMEM((1, 128), F32),
+        pltpu.VMEM(block, jnp.int32),
+        pltpu.VMEM(block, jnp.int32),
+        pltpu.VMEM(block, jnp.int32),
+        pltpu.VMEM((7, *block), F32),
+        pltpu.VMEM((8, wall_free.shape[1]), F32),
+        pltpu.SemaphoreType.DMA((11,)),
         pltpu.VMEM((2, len(MOVING), radial, 16, 128), F32),
         pltpu.VMEM((2, len(STILL), radial, 8, 128), F32),
         pltpu.VMEM((2, 6, 16, 128), F32),
@@ -503,13 +563,9 @@
         pltpu.VMEM((n_th, 2, *block), F32),
         pltpu.VMEM((n_th, 2, *block), F32),
         pltpu.VMEM(block, F32),
-        pltpu.VMEM((128, 384), BF16),
         pltpu.VMEM((128, 128), F32),
         pltpu.VMEM((128, 128), F32),
-        pltpu.VMEM((128, 128), F32),
-        pltpu.VMEM((128, 128), F32),
-        pltpu.VMEM((128, 1024), F32),
-        pltpu.VMEM((128, 1024), F32),
+        wall_block,
         pltpu.SemaphoreType.DMA((STEPS,)),
         pltpu.SemaphoreType.DMA((STEPS,)),
         pltpu.SemaphoreType.DMA((STEPS,)),
@@ -523,20 +579,40 @@
     ]
     field = jax.ShapeDtypeStruct((radial, *block), F32)
     wall = jax.ShapeDtypeStruct(wall_free.shape, F32)
-    return pl.pallas_call(
+    square = jax.ShapeDtypeStruct((128, 128), F32)
+    drug, axial, substep, bound, wide, on_wide, off_wide = pl.pallas_call(
         kernel,
-        out_shape=(field, field, wall, wall),
-        in_specs=[vmem] * 9,
-        out_specs=(vmem,) * 4,
+        out_shape=(
+            field, field, wall, wall, jax.ShapeDtypeStruct((128, 384), BF16), square, square,
+        ),
+        in_specs=[hbm] * 9,
+        out_specs=(vmem,) * 7,
         scratch_shapes=scratch,
         compiler_params=pltpu.CompilerParams(
             collective_id=0, has_side_effects=True, vmem_limit_bytes=40 * 2**20
         ),
     )(
-        populations, wall_free, wall_bound, wall_propagator,
-        bind_on.reshape(1, 128), bind_off.reshape(1, 128),
-        iface_sector.reshape(block), iface_line.reshape(block), strut_mask.reshape(block),
+        *(
+            pltpu.with_memory_space_constraint(x, pltpu.HBM)
+            for x in (
+                populations, wall_free, wall_bound, wall_propagator,
+                bind_on.reshape(1, 128), bind_off.reshape(1, 128),
+                iface_sector.reshape(block), iface_line.reshape(block), strut_mask.reshape(block),
+            )
+        )
     )
+    return pl.pallas_call(
+        finish,
+        out_shape=(field, field, wall, wall),
+        in_specs=[vmem] * 7,
+        out_specs=(hbm,) * 4,
+        scratch_shapes=[
+            wall_block,
+            wall_block,
+            pltpu.SemaphoreType.DMA((2 + 2 * (wall_free.shape[1] // WIDTH),)),
+        ],
+        compiler_params=pltpu.CompilerParams(vmem_limit_bytes=16 * 2**20),
+    )(substep, bound, wide, on_wide, off_wide, drug, axial)
 
 
 def solution(mesh):

time: 59.4 us -> 49.8 us (0.84)
  local copies, waits for them, and re-layouts: 10.6 us -> 0 us
  Pallas kernels: 47.8 us -> 49 us
    unnamed x22 -> x0, local copies, waits for them, and re-layouts: 10.6 us -> none
    pallas_call x1 -> x2, Pallas kernels: 47.8 us -> 49 us  [the longest x1 47.7 us: per_device(): pl.pallas_call(kernel, out_shape=(field, field, wall, wall, jax.ShapeDtyp...]
where the time goes in v1:
time: 49.8 us; the launch traced here: 49.7 us
  Pallas kernels  49 us (98%)
  between operations  0.64 us (1%)
    pallas_call x1, Pallas kernels, per_device(): pl.pallas_call(kernel, out_shape=(field, field, wall, wall, jax.ShapeDtyp...  47.7 us
    pallas_call x1, Pallas kernels, per_device(): pl.pallas_call(finish, out_shape=(field, field, wall, wall), in_specs=[vm...  1.31 us

profile of v1, /device:TPU:1, one launch (start us, length us, event | category | flops | bytes accessed | tf_op | source)
XLA Modules:
  0.0 49.7 jit_solution(7825904080148887041)
XLA Ops:
  0.6 47.7 %shard_map.120 = (f32[16,8,128]{2,1,0:T(8,128)S(1)}, f32[16,8,128]{2,1,0:T(8,128)S(1)}, f32[128,1024]{1,0:T(8,128)S(1)}, f32[128,1024]{1,0:T(8,128)S(1)}, bf16[1...) custom-call(f32[26,16,8,128]{3,2,1,0:T(8,128)} %pops_hbm.1, f32[128,1024]{1,0:T(8,128)} %free_hbm.1, ...), custom_call_target="tpu_custom_call" | custom-call | tf_op jit(solution)/shard_map/pallas_call | solution.py:583
  48.4 1.3 %shard_map.121 = (f32[16,8,128]{2,1,0:T(8,128)}, f32[16,8,128]{2,1,0:T(8,128)}, f32[128,1024]{1,0:T(8,128)}, f32[128,1024]{1,0:T(8,128)}) custom-call(f32[128,1024]{1,0:T(8,128)S(1)} %get-tuple-element.11.substep, f32[128,1024]{1,0:T(8,128)S(1)} %get-tuple-element.12.bound_in, bf16[128,384]{1,0:T(8,128)(2,1)S(1)} %get-tuple-element.13.wide, ...), custom_call_target="tpu_custom_call" | custom-call | tf_op jit(solution)/shard_map/pallas_call | solution.py:604

commit v2 on v1

--- a/solution.py
+++ b/solution.py
@@ -59,11 +59,11 @@
     pops_hbm, free_hbm, bound_hbm, prop_hbm, on_hbm, off_hbm, sector_hbm, line_hbm, strut_hbm,
     drug_out, axial_out, substep, bound, wide, on_wide, off_wide,
     pops, free_in, prop, on_row, off_row, sector, line, strut, first_drug, first_free, load_sems,
-    moving, still, drug_top, drug_now, speed_top, packed, faces, tops,
+    moving, still, drug_top, drug_now, speed_top, packed, faces, incoming, tops,
     onehot_hi, onehot_lo, lanes_lo, code_in, open_row, line_open, line_count, line_strut,
-    table, sums, fixed_out, fixed_in, source,
+    table, sums, first_out, first_in, source,
     from_source, to_surface, propagated,
-    table_send, table_recv, sums_send, sums_recv, fixed_send, fixed_recv,
+    table_send, table_recv, sums_send, sums_recv, first_send, first_recv,
     flow_send, flow_recv, top_send, top_recv,
 ):
     n_ax, n_th = lax.axis_size("ax"), lax.axis_size("th")
@@ -146,6 +146,16 @@
                 result = jnp.where(code == o * 8 + hi, found, result)
         return result
 
+    def table_at(t, o):
+        if t > 0:
+            return table.at[t, o]
+        return first_in.at[o, 2] if o else first_out.at[0, 2]
+
+    def sums_at(t, o):
+        if t > 0:
+            return sums.at[1 if o else 0, t, o]
+        return first_in.at[o, 3] if o else first_out.at[0, 3]
+
     def table_copy(t, o):
         return pltpu.make_async_remote_copy(
             table.at[t, 0], table.at[t, o], table_send.at[t], table_recv.at[t], peer(o), MESH
@@ -156,9 +166,9 @@
             sums.at[0, t, o], sums.at[1, t, o], sums_send.at[t], sums_recv.at[t], peer(o), MESH
         )
 
-    def fixed_copy(o):
+    def first_copy(o):
         return pltpu.make_async_remote_copy(
-            fixed_out.at[o], fixed_in.at[o], fixed_send, fixed_recv, peer(o), MESH
+            first_out.at[o], first_in.at[o], first_send, first_recv, peer(o), MESH
         )
 
     def send_sums(t, surface):
@@ -170,24 +180,24 @@
 
     for load in loads[3:5]:
         load.wait()
-    for c in range(8):
-        table[0, 0, c : c + 1, :] = first_free[0:1, 128 * c : 128 * c + 128]
     strut_own = strut[...].astype(F32)
-    counts = by_line(jnp.ones((8, 128), F32))
-    for o in range(n_th):
-        fixed_out[o, 0] = strut_own
-        fixed_out[o, 1] = counts[8 * o : 8 * o + 8]
     surface = first_drug[0]
     for q in range(20, 26):
         surface = surface + first_drug[q - 19]
+    found = by_line(surface)
+    counts = by_line(jnp.ones((8, 128), F32))
+    for o in range(n_th):
+        first_out[o, 0] = strut_own
+        first_out[o, 1] = counts[8 * o : 8 * o + 8]
+        for c in range(8):
+            first_out[o, 2, c : c + 1, :] = first_free[0:1, 128 * c : 128 * c + 128]
+        first_out[o, 3] = found[8 * o : 8 * o + 8]
+    pl.semaphore_wait(barrier, len(greeted))
+    for o in range(1, n_th):
+        first_copy(o).start()
     for q in range(19, 26):
         drug_now[q - 19] = first_drug[q - 19]
     drug_now[7] = surface
-    pl.semaphore_wait(barrier, len(greeted))
-    for o in range(1, n_th):
-        fixed_copy(o).start()
-        table_copy(0, o).start()
-    send_sums(0, surface)
 
     for load in loads[5:]:
         load.wait()
@@ -217,32 +227,47 @@
             return moving[p, MOVING.index(q), r, 1:9, :]
         return still[p, STILL.index(q), r]
 
-    def rotation(shift):
-        return shift % 128 if isinstance(shift, int) else lax.rem(shift, 128)
-
-    def pulled(t, p, q, r):
+    def spread_faces(t):
+        for side, members in enumerate((Z_UP, Z_DOWN)):
+            for k, q in enumerate(members):
+                first = 8 - VELOCITIES[q][1]
+                face = faces[t, side, first : first + 8, :]
+                incoming[6 * side + k] = pltpu.roll(face, (128 - 16 * k) % 128, 1)
+
+    def pack_faces(t, p):
+        for side, members in enumerate((Z_UP, Z_DOWN)):
+            block = jnp.zeros((8, 128), F32)
+            for k, q in enumerate(members):
+                face = jnp.zeros((8, 128), F32)
+                for r in range(top + 1 if q < 19 else top):
+                    face = jnp.where(lane == r + 1, own(p, q, r)[...], face)
+                block = block + pltpu.roll(face, 16 * k, 1)
+            packed[t, side] = block
+
+    def pulled(p, q, r):
         value = shifted_s(p, q, r)
-        step_z, step_s, _ = VELOCITIES[q]
-        if step_z == 0:
-            return value
-        first = 8 - step_s
-        if step_z == 1:
-            face = faces[t, 0, first : first + 8, :]
-            slot = Z_UP.index(q) * 16 + r
-            face = pltpu.roll(face, rotation(128 - slot), 1)
-            return jnp.where(lane == 0, face, pltpu.roll(value, 1, 1))
-        face = faces[t, 1, first : first + 8, :]
-        slot = Z_DOWN.index(q) * 16 + r
-        face = pltpu.roll(face, rotation(127 - slot), 1)
-        return jnp.where(lane == 127, face, pltpu.roll(value, 127, 1))
-
-    def moved(t, p, q, r, where):
+        if q in Z_UP:
+            value = jnp.where(lane == r + 1, incoming[Z_UP.index(q)], value)
+            return pltpu.roll(value, 127 - r, 1)
+        if q in Z_DOWN:
+            value = jnp.where(lane == r + 1, incoming[6 + Z_DOWN.index(q)], value)
+            return pltpu.roll(value, 126 - r, 1)
+        return value
+
+    def own_plain(p, q, r):
+        if q in Z_UP:
+            return pltpu.roll(own(p, q, r)[...], 126 - r, 1)
+        if q in Z_DOWN:
+            return pltpu.roll(own(p, q, r)[...], 127 - r, 1)
+        return own(p, q, r)[...]
+
+    def moved(p, q, r, where):
         step_r = VELOCITIES[q][2]
         if step_r == 1 and where == "bottom":
-            return pulled(t, p, MIRROR[q], r)
+            return pulled(p, MIRROR[q], r)
         if step_r == -1 and where == "top":
-            return own(p, OPPOSITE[q], r)[...]
-        return pulled(t, p, q, r - step_r)
+            return own_plain(p, OPPOSITE[q], r)
+        return pulled(p, q, r - step_r)
 
     def collide_flow(f):
         d = {q: f[q] - f[q + 1] for q in (1, 3, 5, 7, 9, 11, 13, 15, 17)}
@@ -280,32 +305,30 @@
             post[q + 1] = keep * f[q + 1] + share * (1.0 - odd)
         return post
 
-    def pack(post, r, packs):
-        up, down = packs
-        for k, q in enumerate(Z_UP):
-            if q in post:
-                slot = 16 * k + r
-                up = jnp.where(lane == slot, pltpu.roll(post[q], rotation(slot + 1), 1), up)
-        for k, q in enumerate(Z_DOWN):
-            if q in post:
-                slot = 16 * k + r
-                down = jnp.where(lane == slot, pltpu.roll(post[q], rotation(slot), 1), down)
-        return up, down
-
-    def layer(read, p, r, packs, where):
-        f = {q: read(q, r, where) for q in range(19 if where == "top" else 26)}
-        post, speeds = collide_flow(f)
-        if where == "top":
-            for i in range(3):
-                speed_top[i] = speeds[i]
-        else:
-            total = f[19]
-            for q in range(20, 26):
-                total = total + f[q]
-            post.update(collide_drug(f, total, speeds))
-        for q, value in post.items():
-            own(p, q, r)[...] = value
-        return pack(post, r, packs)
+    def layers(read, p, rows):
+        loaded = []
+        for r, where in rows:
+            members = range(19 if where == "top" else 26)
+            loaded.append({q: read(q, r, where) for q in members})
+        posts = []
+        for (_, where), f in zip(rows, loaded):
+            post, speeds = collide_flow(f)
+            if where == "top":
+                for i in range(3):
+                    speed_top[i] = speeds[i]
+            else:
+                total = f[19]
+                for q in range(20, 26):
+                    total = total + f[q]
+                post.update(collide_drug(f, total, speeds))
+            posts.append(post)
+        for (r, _), post in zip(rows, posts):
+            for q, value in post.items():
+                if q in Z_UP:
+                    value = pltpu.roll(value, r + 2, 1)
+                elif q in Z_DOWN:
+                    value = pltpu.roll(value, r + 1, 1)
+                own(p, q, r)[...] = value
 
     def flow_copies(t, p):
         def copy(src, dst, device, i):
@@ -329,16 +352,20 @@
             ]
         return copies
 
-    def collide_all(t, p, read, bottom):
-        packs = (jnp.zeros((8, 128), F32), jnp.zeros((8, 128), F32))
-        if bottom:
-            packs = layer(read, p, 0, packs, "bottom")
-        packs = lax.fori_loop(
-            1 if bottom else 0, top, lambda r, packs: layer(read, p, r, packs, "middle"), packs
-        )
-        up, down = layer(read, p, top, packs, "top")
-        packed[t, 0] = up
-        packed[t, 1] = down
+    def collide_all(t, p):
+        if t == 0:
+            read = lambda q, r, where: pops[q, r]
+        else:
+            spread_faces(t - 1)
+            read = functools.partial(moved, 1 - p)
+        layers(read, p, [(0, "bottom"), (top, "top")])
+
+        def pair(i, carry):
+            layers(read, p, [(2 * i + 1, "middle"), (2 * i + 2, "middle")])
+            return carry
+
+        lax.fori_loop(0, (top - 1) // 2, pair, 0)
+        pack_faces(t, p)
         for copy in flow_copies(t, p):
             copy.start()
 
@@ -356,8 +383,9 @@
         ]
 
     def wall_flux(t, p):
-        wait_bytes(table.at[t, pl.ds(1, n_th - 1)], table_recv.at[t])
-        free_rows = gathered(lambda o, hi: table[t, o, hi : hi + 1, :])
+        if t > 0:
+            wait_bytes(table.at[t, pl.ds(1, n_th - 1)], table_recv.at[t])
+        free_rows = gathered(lambda o, hi: table_at(t, o)[hi : hi + 1, :])
         surface = drug_now[7]
         flux = open_row[...] * (surface - free_rows)
         lowered = {19: drug_now[0] - 0.25 * flux}
@@ -375,11 +403,12 @@
         own(p, 25, top)[...] = post[25]
 
     def wall_first(t, send):
-        wait_bytes(sums.at[1, t, pl.ds(1, n_th - 1)], sums_recv.at[t])
-        total = sums[0, t, 0]
+        if t > 0:
+            wait_bytes(sums.at[1, t, pl.ds(1, n_th - 1)], sums_recv.at[t])
+        total = sums_at(t, 0)[...]
         for o in range(1, n_th):
-            total = total + sums[1, t, o]
-        flux = line_open[...] * (total - line_count[...] * table[t, 0])
+            total = total + sums_at(t, o)[...]
+        flux = line_open[...] * (total - line_count[...] * table_at(t, 0)[...])
         source[...] = flux + RELEASE_RATE * line_strut[...]
         for c in range(8):
             part = pl.ds(128 * c, 128)
@@ -426,21 +455,22 @@
             copy.wait()
 
     def wait_coupling_sends(t):
+        if t == 0:
+            wait_bytes(first_in.at[pl.ds(1, n_th - 1)], first_send)
+            return
         wait_bytes(table.at[t, pl.ds(1, n_th - 1)], table_send.at[t])
         wait_bytes(sums.at[1, t, pl.ds(1, n_th - 1)], sums_send.at[t])
 
-    collide_all(0, 0, lambda q, r, where: pops[q, r], False)
-    wait_bytes(fixed_in.at[pl.ds(1, n_th - 1)], fixed_recv)
+    collide_all(0, 0)
+    wait_bytes(first_in.at[pl.ds(1, n_th - 1)], first_recv)
     line_strut[...] = strut_own
     line_open[...] = PERMEABILITY * (1.0 - strut_own)
-    count = fixed_out[0, 1]
+    count = first_out[0, 1]
     for o in range(1, n_th):
-        count = count + fixed_in[o, 1]
+        count = count + first_in[o, 1]
     line_count[...] = count
-    fixed_in[0, 0] = strut_own
-    covered = gathered(lambda o, hi: fixed_in[o, 0, hi : hi + 1, :])
+    covered = gathered(lambda o, hi: (first_in if o else first_out)[o, 0, hi : hi + 1, :])
     open_row[...] = PERMEABILITY * (1.0 - covered)
-    wait_bytes(fixed_in.at[pl.ds(1, n_th - 1)], fixed_send)
 
     def wall_side(t, p):
         wait_tops(t, p)
@@ -450,44 +480,43 @@
         drug_now[7] = total
         send_sums(t + 1, total)
 
-    def step(t, carry):
-        p = lax.rem(t, 2)
+    for t in range(STEPS - 1):
+        p = t % 2
         wall_flux(t, p)
         wall_first(t, True)
-        pl.when(p == 1)(lambda: wall_side(t, p))
+        if p == 1:
+            wall_side(t, p)
         wall_second()
         wait_coupling_sends(t)
         wait_flow(t, p)
-        collide_all(t + 1, 1 - p, lambda q, r, where: moved(t, p, q, r, where), True)
-        pl.when(p == 0)(lambda: wall_side(t, p))
-        return carry
-
-    lax.fori_loop(0, STEPS - 1, step, 0)
+        collide_all(t + 1, 1 - p)
+        if p == 0:
+            wall_side(t, p)
 
     t, p = STEPS - 1, (STEPS - 1) % 2
     wall_flux(t, p)
     wait_flow(t, p)
 
-    def result(r, where):
-        f = {q: moved(t, p, q, r, where) for q in Z_UP[:5] + Z_DOWN[:5]}
-        flow = None
-        for q in Z_UP[:5]:
-            term = f[q] - f[OPPOSITE[q]]
-            flow = term if flow is None else flow + term
-        axial_out[r] = flow
-        if where != "top":
-            total = moved(t, p, 19, r, where)
-            for q in range(20, 26):
-                total = total + moved(t, p, q, r, where)
-            drug_out[r] = total
-
-    def result_middle(r, carry):
-        result(r, "middle")
+    def results(rows):
+        for r, where in rows:
+            flow = None
+            for q in Z_UP[:5]:
+                term = moved(p, q, r, where) - moved(p, OPPOSITE[q], r, where)
+                flow = term if flow is None else flow + term
+            axial_out[r] = flow
+            if where != "top":
+                total = moved(p, 19, r, where)
+                for q in range(20, 26):
+                    total = total + moved(p, q, r, where)
+                drug_out[r] = total
+
+    def results_pair(i, carry):
+        results([(2 * i + 1, "middle"), (2 * i + 2, "middle")])
         return carry
 
-    result(0, "bottom")
-    lax.fori_loop(1, top, result_middle, 0)
-    result(top, "top")
+    spread_faces(t)
+    results([(0, "bottom"), (top, "top")])
+    lax.fori_loop(0, (top - 1) // 2, results_pair, 0)
     wall_first(t, False)
     wait_coupling_sends(t)
     wait_tops(t, p)
@@ -549,6 +578,7 @@
         pltpu.VMEM((3, *block), F32),
         pltpu.VMEM((STEPS, 2, *block), F32),
         pltpu.VMEM((STEPS, 2, 24, 128), F32),
+        pltpu.VMEM((12, *block), F32),
         pltpu.VMEM((STEPS, 2, *block), F32),
         pltpu.VMEM((8 * n_th, 1024), BF16),
         pltpu.VMEM((128, 1024), BF16),
@@ -560,8 +590,8 @@
         pltpu.VMEM(block, F32),
         pltpu.VMEM((STEPS, n_th, *block), F32),
         pltpu.VMEM((2, STEPS, n_th, *block), F32),
-        pltpu.VMEM((n_th, 2, *block), F32),
-        pltpu.VMEM((n_th, 2, *block), F32),
+        pltpu.VMEM((n_th, 4, *block), F32),
+        pltpu.VMEM((n_th, 4, *block), F32),
         pltpu.VMEM(block, F32),
         pltpu.VMEM((128, 128), F32),
         pltpu.VMEM((128, 128), F32),

time: 49.8 us -> 44.7 us (0.90)
  Pallas kernels: 49 us -> 43.9 us
    pallas_call x1, Pallas kernels: 47.7 us -> 42.6 us  [per_device(): pl.pallas_call(kernel, out_shape=(field, field, wall, wall, jax.ShapeDtyp...]
where the time goes in v2:
time: 44.7 us; the launch traced here: 44.6 us
  Pallas kernels  43.9 us (98%)
  between operations  0.64 us (1%)
    pallas_call x1, Pallas kernels, per_device(): pl.pallas_call(kernel, out_shape=(field, field, wall, wall, jax.ShapeDtyp...  42.6 us
    pallas_call x1, Pallas kernels, per_device(): pl.pallas_call(finish, out_shape=(field, field, wall, wall), in_specs=[vm...  1.3 us

profile of v2, /device:TPU:1, one launch (start us, length us, event | category | flops | bytes accessed | tf_op | source)
XLA Modules:
  0.0 44.6 jit_solution(1007487970161184023)
XLA Ops:
  0.6 42.6 %shard_map.120 = (f32[16,8,128]{2,1,0:T(8,128)S(1)}, f32[16,8,128]{2,1,0:T(8,128)S(1)}, f32[128,1024]{1,0:T(8,128)S(1)}, f32[128,1024]{1,0:T(8,128)S(1)}, bf16[1...) custom-call(f32[26,16,8,128]{3,2,1,0:T(8,128)} %pops_hbm.1, f32[128,1024]{1,0:T(8,128)} %free_hbm.1, ...), custom_call_target="tpu_custom_call" | custom-call | tf_op jit(solution)/shard_map/pallas_call | solution.py:613
  43.3 1.3 %shard_map.121 = (f32[16,8,128]{2,1,0:T(8,128)}, f32[16,8,128]{2,1,0:T(8,128)}, f32[128,1024]{1,0:T(8,128)}, f32[128,1024]{1,0:T(8,128)}) custom-call(f32[128,1024]{1,0:T(8,128)S(1)} %get-tuple-element.11.substep, f32[128,1024]{1,0:T(8,128)S(1)} %get-tuple-element.12.bound_in, bf16[128,384]{1,0:T(8,128)(2,1)S(1)} %get-tuple-element.13.wide, ...), custom_call_target="tpu_custom_call" | custom-call | tf_op jit(solution)/shard_map/pallas_call | solution.py:634

commit v3 on v2

--- a/solution.py
+++ b/solution.py
@@ -64,7 +64,7 @@
     table, sums, first_out, first_in, source,
     from_source, to_surface, propagated,
     table_send, table_recv, sums_send, sums_recv, first_send, first_recv,
-    flow_send, flow_recv, top_send, top_recv,
+    edge_send, edge_recv, flow_send, flow_recv, top_send, top_recv,
 ):
     n_ax, n_th = lax.axis_size("ax"), lax.axis_size("th")
     ax, th = lax.axis_index("ax"), lax.axis_index("th")
@@ -336,21 +336,31 @@
                 src, dst, flow_send.at[t, i], flow_recv.at[t, i], device, MESH
             )
 
-        up, down = (ax, th_up), (ax, th_down)
-        copies = [
-            copy(moving.at[p, 0:5, :, 15, :], moving.at[p, 0:5, :, 7, :], up, 0),
-            copy(moving.at[p, 6:11, :, 0, :], moving.at[p, 6:11, :, 8, :], down, 1),
-            copy(moving.at[p, 5, 0:top, 15, :], moving.at[p, 5, 0:top, 7, :], up, 2),
-            copy(moving.at[p, 11, 0:top, 0, :], moving.at[p, 11, 0:top, 8, :], down, 3),
-        ]
+        copies = []
         for side, to in ((0, ax_up), (1, ax_down)):
-            i = 4 + 3 * side
+            i = 3 * side
             copies += [
                 copy(packed.at[t, side], faces.at[t, side, 8:16, :], (to, th), i),
                 copy(packed.at[t, side, 7:8, :], faces.at[t, side, 7:8, :], (to, th_up), i + 1),
                 copy(packed.at[t, side, 0:1, :], faces.at[t, side, 16:17, :], (to, th_down), i + 2),
             ]
         return copies
+
+    def send_edges(t, p, r, count, members):
+        rows = pl.ds(r, count)
+        for side, first, src, dst, to in ((0, 0, 15, 7, th_up), (1, 6, 0, 8, th_down)):
+            movers = pl.ds(first, members)
+            pltpu.make_async_remote_copy(
+                moving.at[p, movers, rows, src, :], moving.at[p, movers, rows, dst, :],
+                edge_send.at[t, side], edge_recv.at[t, side], (ax, to), MESH,
+            ).start()
+
+    def wait_edges(t):
+        all_rows = pops.at[0:19, 0:5, 0, :]
+        assert 19 * 5 == 6 * top + 5
+        for side in range(2):
+            wait_bytes(all_rows, edge_send.at[t, side])
+            wait_bytes(all_rows, edge_recv.at[t, side])
 
     def collide_all(t, p):
         if t == 0:
@@ -359,9 +369,12 @@
             spread_faces(t - 1)
             read = functools.partial(moved, 1 - p)
         layers(read, p, [(0, "bottom"), (top, "top")])
+        send_edges(t, p, 0, 1, 6)
+        send_edges(t, p, top, 1, 5)
 
         def pair(i, carry):
             layers(read, p, [(2 * i + 1, "middle"), (2 * i + 2, "middle")])
+            send_edges(t, p, 2 * i + 1, 2, 6)
             return carry
 
         lax.fori_loop(0, (top - 1) // 2, pair, 0)
@@ -451,6 +464,7 @@
             copy.wait()
 
     def wait_flow(t, p):
+        wait_edges(t)
         for copy in flow_copies(t, p):
             copy.wait()
 
@@ -602,8 +616,10 @@
         pltpu.SemaphoreType.DMA((STEPS,)),
         pltpu.SemaphoreType.DMA,
         pltpu.SemaphoreType.DMA,
-        pltpu.SemaphoreType.DMA((STEPS, 10)),
-        pltpu.SemaphoreType.DMA((STEPS, 10)),
+        pltpu.SemaphoreType.DMA((STEPS, 2)),
+        pltpu.SemaphoreType.DMA((STEPS, 2)),
+        pltpu.SemaphoreType.DMA((STEPS, 6)),
+        pltpu.SemaphoreType.DMA((STEPS, 6)),
         pltpu.SemaphoreType.DMA((STEPS, 4)),
         pltpu.SemaphoreType.DMA((STEPS, 4)),
     ]

time: 44.7 us -> 43.3 us (0.969)
  Pallas kernels: 43.9 us -> 42.6 us
    pallas_call x1, Pallas kernels: 42.6 us -> 41.3 us  [per_device(): pl.pallas_call(kernel, out_shape=(field, field, wall, wall, jax.ShapeDtyp...]
where the time goes in v3:
time: 43.3 us; the launch traced here: 43.2 us
  Pallas kernels  42.6 us (98%)
  between operations  0.64 us (1%)
    pallas_call x1, Pallas kernels, per_device(): pl.pallas_call(kernel, out_shape=(field, field, wall, wall, jax.ShapeDtyp...  41.3 us
    pallas_call x1, Pallas kernels, per_device(): pl.pallas_call(finish, out_shape=(field, field, wall, wall), in_specs=[vm...  1.31 us

profile of v3, /device:TPU:1, one launch (start us, length us, event | category | flops | bytes accessed | tf_op | source)
XLA Modules:
  0.0 43.2 jit_solution(14919892701679133637)
XLA Ops:
  0.6 41.3 %shard_map.120 = (f32[16,8,128]{2,1,0:T(8,128)S(1)}, f32[16,8,128]{2,1,0:T(8,128)S(1)}, f32[128,1024]{1,0:T(8,128)S(1)}, f32[128,1024]{1,0:T(8,128)S(1)}, bf16[1...) custom-call(f32[26,16,8,128]{3,2,1,0:T(8,128)} %pops_hbm.1, f32[128,1024]{1,0:T(8,128)} %free_hbm.1, ...), custom_call_target="tpu_custom_call" | custom-call | tf_op jit(solution)/shard_map/pallas_call | solution.py:629
  41.9 1.3 %shard_map.121 = (f32[16,8,128]{2,1,0:T(8,128)}, f32[16,8,128]{2,1,0:T(8,128)}, f32[128,1024]{1,0:T(8,128)}, f32[128,1024]{1,0:T(8,128)}) custom-call(f32[128,1024]{1,0:T(8,128)S(1)} %get-tuple-element.11.substep, f32[128,1024]{1,0:T(8,128)S(1)} %get-tuple-element.12.bound_in, bf16[128,384]{1,0:T(8,128)(2,1)S(1)} %get-tuple-element.13.wide, ...), custom_call_target="tpu_custom_call" | custom-call | tf_op jit(solution)/shard_map/pallas_call | solution.py:650

commit v4 on v3

--- a/solution.py
+++ b/solution.py
@@ -82,7 +82,8 @@
         (ax_up, th_up), (ax_up, th_down), (ax_down, th_up), (ax_down, th_down),
     ]
     barrier = pltpu.get_barrier_semaphore()
-    greeted = [peer(o) for o in range(1, n_th)] + beside
+    far_first = sorted(range(1, n_th), key=lambda o: -min(o, n_th - o))
+    greeted = [peer(o) for o in far_first] + beside
     for device in greeted:
         pl.semaphore_signal(barrier, inc=1, device_id=device, device_id_type=MESH)
 
@@ -175,7 +176,7 @@
         found = by_line(surface)
         for o in range(n_th):
             sums[0, t, o] = found[8 * o : 8 * o + 8]
-        for o in range(1, n_th):
+        for o in far_first:
             sums_copy(t, o).start()
 
     for load in loads[3:5]:
@@ -193,7 +194,7 @@
             first_out[o, 2, c : c + 1, :] = first_free[0:1, 128 * c : 128 * c + 128]
         first_out[o, 3] = found[8 * o : 8 * o + 8]
     pl.semaphore_wait(barrier, len(greeted))
-    for o in range(1, n_th):
+    for o in far_first:
         first_copy(o).start()
     for q in range(19, 26):
         drug_now[q - 19] = first_drug[q - 19]
@@ -434,7 +435,7 @@
                 x, _ = react(x, b[0:1, :], on_wide[0:1, :], off_wide[0:1, :])
                 table[t + 1, 0, c : c + 1, :] = x
         if send:
-            for o in range(1, n_th):
+            for o in far_first:
                 table_copy(t + 1, o).start()
 
     def wall_second():

time: 43.3 us -> 42.5 us (0.982)
  Pallas kernels: 42.6 us -> 41.7 us
    pallas_call x1, Pallas kernels: 41.3 us -> 40.4 us  [per_device(): pl.pallas_call(kernel, out_shape=(field, field, wall, wall, jax.ShapeDtyp...]
where the time goes in v4:
time: 42.5 us; the launch traced here: 42.4 us
  Pallas kernels  41.7 us (98%)
  between operations  0.64 us (2%)
    pallas_call x1, Pallas kernels, per_device(): pl.pallas_call(kernel, out_shape=(field, field, wall, wall, jax.ShapeDtyp...  40.4 us
    pallas_call x1, Pallas kernels, per_device(): pl.pallas_call(finish, out_shape=(field, field, wall, wall), in_specs=[vm...  1.3 us

profile of v4, /device:TPU:1, one launch (start us, length us, event | category | flops | bytes accessed | tf_op | source)
XLA Modules:
  0.0 42.4 jit_solution(8152719794306746330)
XLA Ops:
  0.6 40.4 %shard_map.120 = (f32[16,8,128]{2,1,0:T(8,128)S(1)}, f32[16,8,128]{2,1,0:T(8,128)S(1)}, f32[128,1024]{1,0:T(8,128)S(1)}, f32[128,1024]{1,0:T(8,128)S(1)}, bf16[1...) custom-call(f32[26,16,8,128]{3,2,1,0:T(8,128)} %pops_hbm.1, f32[128,1024]{1,0:T(8,128)} %free_hbm.1, ...), custom_call_target="tpu_custom_call" | custom-call | tf_op jit(solution)/shard_map/pallas_call | solution.py:630
  41.1 1.3 %shard_map.121 = (f32[16,8,128]{2,1,0:T(8,128)}, f32[16,8,128]{2,1,0:T(8,128)}, f32[128,1024]{1,0:T(8,128)}, f32[128,1024]{1,0:T(8,128)}) custom-call(f32[128,1024]{1,0:T(8,128)S(1)} %get-tuple-element.11.substep, f32[128,1024]{1,0:T(8,128)S(1)} %get-tuple-element.12.bound_in, bf16[128,384]{1,0:T(8,128)(2,1)S(1)} %get-tuple-element.13.wide, ...), custom_call_target="tpu_custom_call" | custom-call | tf_op jit(solution)/shard_map/pallas_call | solution.py:651

commit v5 on v4

--- a/solution.py
+++ b/solution.py
@@ -62,7 +62,7 @@
     moving, still, drug_top, drug_now, speed_top, packed, faces, incoming, tops,
     onehot_hi, onehot_lo, lanes_lo, code_in, open_row, line_open, line_count, line_strut,
     table, sums, first_out, first_in, source,
-    from_source, to_surface, propagated,
+    from_source, to_surface, through, response, propagated,
     table_send, table_recv, sums_send, sums_recv, first_send, first_recv,
     edge_send, edge_recv, flow_send, flow_recv, top_send, top_recv,
 ):
@@ -423,20 +423,34 @@
         for o in range(1, n_th):
             total = total + sums_at(t, o)[...]
         flux = line_open[...] * (total - line_count[...] * table_at(t, 0)[...])
-        source[...] = flux + RELEASE_RATE * line_strut[...]
+        from_lines = flux + RELEASE_RATE * line_strut[...]
+        source[...] = from_lines
+        if send:
+            x = response[0] + response[1] * from_lines
+            b = response[2] + response[3] * from_lines
+            x, _ = react(x, b, on_wide[0:1, :], off_wide[0:1, :])
+            table[t + 1, 0] = x
+            for o in far_first:
+                table_copy(t + 1, o).start()
         for c in range(8):
             part = pl.ds(128 * c, 128)
             x = propagated[:, part] + from_source[...] * source[c : c + 1, :]
             x, b = react(x, bound[:, part], on_wide[...], off_wide[...])
             substep[:, part] = x
             bound[:, part] = b
-            if send:
-                x = jnp.sum(to_surface[...] * x, axis=0, keepdims=True)
-                x, _ = react(x, b[0:1, :], on_wide[0:1, :], off_wide[0:1, :])
-                table[t + 1, 0, c : c + 1, :] = x
-        if send:
-            for o in far_first:
-                table_copy(t + 1, o).start()
+
+    def respond():
+        for c in range(8):
+            part = pl.ds(128 * c, 128)
+            x, b = propagated[:, part], bound[:, part]
+            left = 1.0 - on_wide[...] * (1.0 - b)
+            still_free = to_surface[...] * (x * left + off_wide[...] * b)
+            row = pl.ds(c, 1)
+            response[0, row, :] = jnp.sum(still_free, axis=0, keepdims=True)
+            response[1, row, :] = jnp.sum(through[...] * left, axis=0, keepdims=True)
+            on, off, x, b = on_wide[0:1, :], off_wide[0:1, :], x[0:1, :], b[0:1, :]
+            response[2, row, :] = react(x, b, on, off)[1]
+            response[3, row, :] = on * from_source[0:1, :] * (1.0 - b)
 
     def wall_second():
         wide_on = jnp.concatenate([on_wide[...]] * (WIDTH // 128), axis=1)
@@ -476,7 +490,9 @@
         wait_bytes(table.at[t, pl.ds(1, n_th - 1)], table_send.at[t])
         wait_bytes(sums.at[1, t, pl.ds(1, n_th - 1)], sums_send.at[t])
 
+    through[...] = to_surface[...] * from_source[...]
     collide_all(0, 0)
+    respond()
     wait_bytes(first_in.at[pl.ds(1, n_th - 1)], first_recv)
     line_strut[...] = strut_own
     line_open[...] = PERMEABILITY * (1.0 - strut_own)
@@ -498,15 +514,20 @@
     for t in range(STEPS - 1):
         p = t % 2
         wall_flux(t, p)
+        if p == 1:
+            wait_flow(t, p)
+            collide_all(t + 1, 1 - p)
         wall_first(t, True)
         if p == 1:
             wall_side(t, p)
         wall_second()
         wait_coupling_sends(t)
-        wait_flow(t, p)
-        collide_all(t + 1, 1 - p)
         if p == 0:
+            wait_flow(t, p)
+            collide_all(t + 1, 1 - p)
             wall_side(t, p)
+        if t < STEPS - 2:
+            respond()
 
     t, p = STEPS - 1, (STEPS - 1) % 2
     wall_flux(t, p)
@@ -610,6 +631,8 @@
         pltpu.VMEM(block, F32),
         pltpu.VMEM((128, 128), F32),
         pltpu.VMEM((128, 128), F32),
+        pltpu.VMEM((128, 128), F32),
+        pltpu.VMEM((4, *block), F32),
         wall_block,
         pltpu.SemaphoreType.DMA((STEPS,)),
         pltpu.SemaphoreType.DMA((STEPS,)),

time: 42.5 us -> 41.9 us (0.986)
  Pallas kernels: 41.7 us -> 41.2 us
    pallas_call x1, Pallas kernels: 40.4 us -> 39.9 us  [per_device(): pl.pallas_call(kernel, out_shape=(field, field, wall, wall, jax.ShapeDtyp...]
where the time goes in v5:
time: 41.9 us; the launch traced here: 41.8 us
  Pallas kernels  41.2 us (98%)
  between operations  0.64 us (2%)
    pallas_call x1, Pallas kernels, per_device(): pl.pallas_call(kernel, out_shape=(field, field, wall, wall, jax.ShapeDtyp...  39.9 us
    pallas_call x1, Pallas kernels, per_device(): pl.pallas_call(finish, out_shape=(field, field, wall, wall), in_specs=[vm...  1.31 us

profile of v5, /device:TPU:1, one launch (start us, length us, event | category | flops | bytes accessed | tf_op | source)
XLA Modules:
  0.0 41.8 jit_solution(1162245005366043956)
XLA Ops:
  0.6 39.9 %shard_map.120 = (f32[16,8,128]{2,1,0:T(8,128)S(1)}, f32[16,8,128]{2,1,0:T(8,128)S(1)}, f32[128,1024]{1,0:T(8,128)S(1)}, f32[128,1024]{1,0:T(8,128)S(1)}, bf16[1...) custom-call(f32[26,16,8,128]{3,2,1,0:T(8,128)} %pops_hbm.1, f32[128,1024]{1,0:T(8,128)} %free_hbm.1, ...), custom_call_target="tpu_custom_call" | custom-call | tf_op jit(solution)/shard_map/pallas_call | solution.py:653
  40.5 1.3 %shard_map.121 = (f32[16,8,128]{2,1,0:T(8,128)}, f32[16,8,128]{2,1,0:T(8,128)}, f32[128,1024]{1,0:T(8,128)}, f32[128,1024]{1,0:T(8,128)}) custom-call(f32[128,1024]{1,0:T(8,128)S(1)} %get-tuple-element.11.substep, f32[128,1024]{1,0:T(8,128)S(1)} %get-tuple-element.12.bound_in, bf16[128,384]{1,0:T(8,128)(2,1)S(1)} %get-tuple-element.13.wide, ...), custom_call_target="tpu_custom_call" | custom-call | tf_op jit(solution)/shard_map/pallas_call | solution.py:674
